TPU v7x, 256 devices: a whole 4x4x8 slice. The times are simulated.
256 devices in a mesh: rep: 16 (over z_hi, x, core), fsdp: 16 (over z_lo, y).
Axes of the slice: x: 4, y: 4, z: 8 (z_hi: 2, z_lo: 4; z = z_hi * 4 + z_lo), core: 2. Of those that a mesh axis runs over, the one named last changes fastest.
Arguments:
- hidden: bfloat16 [16, 7168, 2048], P('rep', 'fsdp'), may hold values from -6 to 6
- target: bfloat16 [16, 2048, 2048], P('rep', 'fsdp'), may hold values from -6 to 6
- weights: bfloat16 [16, 7168, 2048], P('rep', 'fsdp'), may hold values from -0.0625 to 0.0625
- moment: bfloat16 [16, 7168, 2048], P('rep', 'fsdp'), may hold values from -0.75 to 0.75
- second: bfloat16 [16, 7168, 2048], P('rep', 'fsdp'), may hold values from 0.0024871826 to 0.25
- round_index: int32 [1], replicated, may hold values from 0 to 999
Outputs:
- averaged: bfloat16 [16, 7168, 2048], P('rep', 'fsdp')
- new_moment: bfloat16 [16, 7168, 2048], P('rep', 'fsdp')
- hidden_grad: bfloat16 [16, 7168, 2048], P('rep', 'fsdp')
Inputs may be any that keep to these rules, and one draw needn't show every extreme that they name: The partner group lies 2 ** (round_index modulo 3) groups away in the XOR sense.
All inputs are finite; a program needn't handle non-finite values.
Results may differ from a plain program's by a relative error of at most 0.02.
Values may be sent and summed in bfloat16 or wider, within the bound.
A program may use at most 128 MiB of HBM per device.

v0:
```python
from functools import partial

import jax
import jax.numpy as jnp
from jax import lax
from jax.sharding import PartitionSpec as P

corr_first = 0.9999734386011124
corr_second = 0.994079470779666


def shortened(x):
    return jax.tree.map(lambda a: a.astype(jnp.bfloat16) if a.dtype == jnp.float32 else a, x)


def partner(x, axis, bit):
    return lax.ppermute(x, axis, [(i, i ^ 1 << bit) for i in range(lax.axis_size(axis))])


def adamw_rows(weight_now, moment_now, second_now, grad):
    weight_full = weight_now.astype(jnp.float32)
    first = 0.9 * moment_now.astype(jnp.float32) + 0.1 * grad
    secnd = 0.95 * second_now.astype(jnp.float32) + 0.05 * grad * grad
    stepped = first / corr_first / (jnp.sqrt(secnd / corr_second) + 1e-08)
    updated = (weight_full - 0.02 * (stepped + 0.1 * weight_full)).astype(jnp.bfloat16)
    return (updated, first.astype(jnp.bfloat16))


def whole_swap(values, level):
    return jax.tree.map(
        lambda part, own: part.astype(own.dtype), partner(shortened(values), "rep", level), values
    )


def with_partner(values, round_index, helper):
    levels = min(3, lax.axis_size("rep") // 2)
    branches = [partial(helper, level=level) for level in range(levels)]
    chosen = jnp.remainder(round_index[0], levels)
    partner_values = lax.switch(chosen, branches, values)
    return ((values.astype(jnp.float32) + partner_values.astype(jnp.float32)) * 0.5).astype(
        jnp.bfloat16
    )


def local(hidden, target, weights, moment, second, round_index):
    hidden_cols = hidden[0]
    weight_now = weights[0]
    group_tokens = hidden_cols.shape[1]
    contract_first = (((0,), (0,)), ((), ()))
    contract_last = (((1,), (1,)), ((), ()))
    partial_out = lax.dot_general(
        hidden_cols, weight_now, contract_first, preferred_element_type=jnp.float32
    )
    out_rows = lax.psum_scatter(
        partial_out.astype(jnp.bfloat16), "fsdp", scatter_dimension=0, tiled=True
    ).astype(jnp.float32)
    error = (out_rows - target[0].astype(jnp.float32)).astype(jnp.bfloat16)
    all_errors = lax.all_gather(error, "fsdp", axis=0, tiled=True)
    grad_sum = jnp.dot(hidden_cols, all_errors, preferred_element_type=jnp.float32)
    hidden_full = lax.dot_general(
        weight_now, all_errors, contract_last, preferred_element_type=jnp.float32
    )
    hidden_grad = hidden_full.astype(jnp.bfloat16)
    grad = grad_sum / group_tokens
    updated, first_new = adamw_rows(weight_now, moment[0], second[0], grad)
    averaged = with_partner(updated, round_index, whole_swap)
    return (averaged[None], first_new[None], hidden_grad[None])


def solution(mesh):
    in_specs = (
        P("rep", "fsdp", None),
        P("rep", "fsdp", None),
        P("rep", "fsdp", None),
        P("rep", "fsdp", None),
        P("rep", "fsdp", None),
        P(),
    )
    out_specs = (P("rep", "fsdp", None), P("rep", "fsdp", None), P("rep", "fsdp", None))
    return jax.shard_map(local, mesh=mesh, in_specs=in_specs, out_specs=out_specs, check_vma=False)
```

profile of v0, /device:TPU:4, one launch (start us, length us, event | category | flops | bytes accessed | tf_op | source)
XLA Modules:
  0.0 305.0 jit_solution(7531602534304804780)
XLA Ops:
  7.2 0.0 copy-start
  7.2 0.0 reduce-scatter.2.cloned.1.call-start
  7.2 1.4 copy-done
  8.7 8.2 %convolution_convert_fusion = bf16[2048,2048]{1,0:T(8,128)(2,1)} fusion(bf16[1,448,2048]{2,1,0:T(8,128)(2,1)S(1)} %copy-done, bf16[1,448,2048]{2,1,0:T(8,128)(2,1)} %param.11), kind=kOutput, calls=%fused_computation | convolution fusion | flops 3762290688 | bytes 12058624 | tf_op jit(solution)/shard_map/dot_general | solution.py:51
  16.9 0.0 copy-start.2
  16.9 0.0 reduce-scatter.2.cloned.1.call-update
  16.9 0.0 all-gather.2.cloned.1.call-start
  17.0 110.1 %reduce-scatter.2.cloned.1.call-done = bf16[128,2048]{1,0:T(8,128)(2,1)} async-done(((bf16[2048,2048]{1,0:T(8,128)(2,1)}), bf16[128,2048]{1,0:T(8,128)(2,1)}) %reduce-scatter.2.cloned.1.call-update) | async-done | bytes 524304 | tf_op jit(solution)/shard_map/reduce_scatter | solution.py:54
  127.1 0.0 copy-done.2
  127.1 2.0 fusion.16
  129.0 0.0 all-gather.2.cloned.1.call-update
  129.7 98.7 %all-gather.2.cloned.1.call-done = bf16[2048,2048]{1,0:T(8,128)(2,1)} async-done(((bf16[128,2048]{1,0:T(8,128)(2,1)}), bf16[2048,2048]{1,0:T(8,128)(2,1)}) %all-gather.2.cloned.1.call-update) | async-done | bytes 8388624 | tf_op jit(solution)/shard_map/all_gather | solution.py:58
  228.5 12.9 %fusion.9 = (bf16[1,448,2048]{2,1,0:T(8,128)(2,1)}, bf16[448,2048]{1,0:T(8,128)(2,1)S(1)}) fusion(bf16[1,448,2048]{2,1,0:T(8,128)(2,1)} %param.12, bf16[1,448,2048]{2,1,0:T(8,128)(2,1)} %param.13, bf16[1,448,2048]{2,1,0:T(8,128)(2,1)} %param.11, bf16[2048,2048]{1,0:T(8,128)(2,1)} %all-gather.2.cloned.1.call-done, bf16[1,448,2048]{2,1,0:T(8,128)(2,1)S(1)} %copy-done), kind=kOutput, calls=%fused_computation.16 | convolution fusion | flops 3777363968 | bytes 19398656 | tf_op jit(solution)/shard_map/dot_general | solution.py:59
  241.3 0.0 copy-start.1
  241.3 1.2 copy-done.1
  242.5 41.9 %conditional.4 = (bf16[448,2048]{1,0:T(8,128)(2,1)}) conditional(s32[]{:T(128)} %clamp.3, bf16[448,2048]{1,0:T(8,128)(2,1)S(1)} %get-tuple-element.17, bf16[448,2048]{1,0:T(8,128)(2,1)S(1)} %get-tuple-element.17, bf16[448,2048]{1,0:T(8,128)(2,1)S(1)} %get-tuple-element.17), branch_computations={%region_1.2_spmd, %region_2.3_spmd, %region_3.4_spmd} | conditional | bytes 7340080
  242.5 1.2 collective-permute-start.1
  243.7 40.7 %collective-permute-done.1 = bf16[448,2048]{1,0:T(8,128)(2,1)} collective-permute-done((bf16[448,2048]{1,0:T(8,128)(2,1)S(1)}, bf16[448,2048]{1,0:T(8,128)(2,1)}, u32[]{:S(2)}, u32[]{:S(2)}) %collective-permute-start.1) | collective-permute-done | bytes 1835040 | tf_op jit(solution)/shard_map/cond/branch_1_fun/ppermute | solution.py:17
  284.4 0.0 copy-start.3
  284.4 4.2 %fusion.10 = bf16[1,448,2048]{2,1,0:T(8,128)(2,1)} fusion(bf16[448,2048]{1,0:T(8,128)(2,1)} %get-tuple-element.18, bf16[448,2048]{1,0:T(8,128)(2,1)} %copy-done.1), kind=kLoop, calls=%fused_computation.17 | loop fusion | flops 4587520 | bytes 5505024 | tf_op jit(solution)/shard_map/broadcast_in_dim | solution.py:67
  288.6 0.0 copy-done.3
  288.6 9.6 %fusion.8 = bf16[1,448,2048]{2,1,0:T(8,128)(2,1)} fusion(bf16[2048,2048]{1,0:T(8,128)(2,1)} %all-gather.2.cloned.1.call-done, bf16[1,448,2048]{2,1,0:T(8,128)(2,1)S(1)} %copy-done.3), kind=kOutput, calls=%fused_computation.15 | convolution fusion | flops 3759013888 | bytes 12058624 | tf_op jit(solution)/shard_map/dot_general | solution.py:60
Async XLA Ops:
  7.2 1.5 copy-start
  7.2 119.9 %reduce-scatter.2.cloned.1.call-start = ((), (), s32[]{:S(2)}) async-start(), calls=%async_computation.1 | async-start | bytes 8912896 | tf_op jit(solution)/shard_map/reduce_scatter | solution.py:54
  16.9 110.2 %copy-start.2 = (bf16[1,128,2048]{2,1,0:T(8,128)(2,1)S(1)}, bf16[1,128,2048]{2,1,0:T(8,128)(2,1)}, u32[]{:S(2)}) copy-start(bf16[1,128,2048]{2,1,0:T(8,128)(2,1)} %param.10) | copy-start | bytes 1572868
  16.9 211.5 %all-gather.2.cloned.1.call-start = ((), (), s32[]{:S(2)}) async-start(), calls=%async_computation.2 | async-start | bytes 8912896 | tf_op jit(solution)/shard_map/all_gather | solution.py:58
  241.3 1.2 copy-start.1
  242.5 41.9 %collective-permute-start.1 = (bf16[448,2048]{1,0:T(8,128)(2,1)S(1)}, bf16[448,2048]{1,0:T(8,128)(2,1)}, u32[]{:S(2)}, u32[]{:S(2)}) collective-permute-start(bf16[448,2048]{1,0:T(8,128)(2,1)S(1)} %param.1), channel_id=1, source_target_pairs={{0,32},{16,48},{32,0},{48,16},{64,96},{80,112},{96,64},{112,80},{1... | collective-permute-start | bytes 5505032 | tf_op jit(solution)/shard_map/cond/branch_1_fun/ppermute | solution.py:17
  284.4 4.2 %copy-start.3 = (bf16[1,448,2048]{2,1,0:T(8,128)(2,1)S(1)}, bf16[1,448,2048]{2,1,0:T(8,128)(2,1)}, u32[]{:S(2)}) copy-start(bf16[1,448,2048]{2,1,0:T(8,128)(2,1)} %param.11) | copy-start | bytes 5505028
Sparse Core Ops, SparseCore 0:
  17.1 109.9 reduce-scatter.1
  129.4 98.9 all-gather.1
where the time goes:
time: 305 us
  waiting for transfers between devices  250 us (82%)
  matrix products  30.7 us (10%)
  between operations  14.7 us (5%)
  other arithmetic  6.13 us (2%)
    reduce_scatter x1, waiting for transfers between devices, local(): lax.psum_scatter(partial_out.astype(jnp.bfloat16), 'fsdp', scatter_dimens...  110 us
    all_gather x1, waiting for transfers between devices, local(): all_errors = lax.all_gather(error, 'fsdp', axis=0, tiled=True)  98.7 us
    ppermute x1, waiting for transfers between devices, partner(): lax.ppermute(x, axis, [(i, i ^ 1 << bit) for i in range(lax.axis_size(axi...  40.7 us
    dot_general x1, matrix products, local(): jnp.dot(hidden_cols, all_errors, preferred_element_type=jnp.float32)  12.9 us
    dot_general x1, matrix products, local(): lax.dot_general(weight_now, all_errors, contract_last, preferred_element_...  9.62 us
    dot_general x1, matrix products, local(): lax.dot_general(hidden_cols, weight_now, contract_first, preferred_elemen...  8.24 us
  transfers between devices with their start and end apart: 3, of which 3 were waited for; matrix products, arithmetic and copies ran while one was open for 0% of the time, Pallas kernels for 0%

commit v1 on v0

v1 whole, which is shorter than its diff:
```python
import functools

import jax
import jax.numpy as jnp
from jax import lax
from jax.experimental import pallas as pl
from jax.experimental.pallas import tpu as pltpu
from jax.sharding import PartitionSpec as P

MESH = pl.DeviceIdType.MESH
BF16 = jnp.bfloat16
F32 = jnp.float32
corr_first = 0.9999734386011124
corr_second = 0.994079470779666
NY = 4
NZ = 4
WIDTH = 128
LEVELS = 3


def f32(x):
    return x.astype(F32)


def kernel(
    level,
    h_hbm,
    t_hbm,
    w_hbm,
    m_hbm,
    s_hbm,
    avg_hbm,
    nm_hbm,
    hg_hbm,
    hid,
    hid_t,
    wts,
    mom,
    sec,
    tgt,
    part,
    got1,
    got2,
    got3,
    err,
    acc,
    upd,
    got6,
    avg,
    nmo,
    hgr,
    in_sem,
    out_sem,
    send_sem,
    recv_sem,
):
    chunks, units, width = wts.shape
    rows = tgt.shape[1]
    tokens = NY * NZ * rows
    block = NY * rows
    last = chunks - 1

    fs = lax.axis_index("fsdp")
    rep = lax.axis_index("rep")
    z = fs // NY
    y = fs % NY
    bit = 1 << level
    mate = {"rep": rep + bit * (1 - 2 * ((rep // bit) % 2))}
    yr = (y + 1) % NY
    yl = (y + 3) % NY
    y2 = (y + 2) % NY
    right = {"fsdp": z * NY + yr}
    left = {"fsdp": z * NY + yl}
    zs = [(z + k) % NZ for k in range(NZ)]
    zdev = [{"fsdp": zz * NY + y} for zz in zs]

    barrier = pltpu.get_barrier_semaphore()
    peers = [right, left, zdev[1], zdev[2], zdev[3], mate]
    for peer in peers:
        pl.semaphore_signal(barrier, inc=1, device_id=peer, device_id_type=MESH)

    def cols(c):
        return pl.ds(pl.multiple_of(c * width, width), width)

    sources = ((w_hbm, wts), (t_hbm, tgt), (m_hbm, mom), (s_hbm, sec))
    sinks = ((nmo, nm_hbm), (avg, avg_hbm))

    def load(c, j):
        src, dst = sources[j]
        return pltpu.make_async_copy(src.at[:, cols(c)], dst.at[c], in_sem.at[c, j])

    def write(c, j):
        src, dst = sinks[j]
        return pltpu.make_async_copy(src.at[c], dst.at[:, cols(c)], out_sem.at[c, j])

    load_h = pltpu.make_async_copy(h_hbm, hid, in_sem.at[0, 4])
    write_h = pltpu.make_async_copy(hgr, hg_hbm, out_sem.at[0, 2])

    def remote(src, dst, c, j, dev):
        return pltpu.make_async_remote_copy(
            src_ref=src,
            dst_ref=dst,
            send_sem=send_sem.at[c, j],
            recv_sem=recv_sem.at[c, j],
            device_id=dev,
            device_id_type=MESH,
        )

    lo = pl.ds(0, NZ // 2)
    hi = pl.ds(NZ // 2, NZ // 2)

    def ry_one(c):
        return [
            remote(part.at[c, lo, y2], got1.at[c, 0], c, 0, right),
            remote(part.at[c, hi, y2], got1.at[c, 1], c, 1, left),
        ]

    def ry_two(c):
        return [
            remote(part.at[c, :, yr], got2.at[c, 0], c, 2, right),
            remote(part.at[c, :, yl], got2.at[c, 1], c, 3, left),
        ]

    def rz(c):
        return [
            remote(part.at[c, zs[k], y], got3.at[c, k - 1], c, 3 + k, zdev[k])
            for k in (2, 1, 3)
        ]

    def gz(c):
        return [
            remote(err.at[c, z, y], err.at[c, z, y], c, 6 + k, zdev[k])
            for k in (2, 1, 3)
        ]

    def gy_one(c):
        return [
            remote(err.at[c, :, y], err.at[c, :, y], c, 10, right),
            remote(err.at[c, :, y], err.at[c, :, y], c, 11, left),
        ]

    def gy_two(c):
        return [
            remote(err.at[c, lo, yl], err.at[c, lo, yl], c, 12, right),
            remote(err.at[c, hi, yr], err.at[c, hi, yr], c, 13, left),
        ]

    def swap(c):
        return [remote(upd.at[c], got6.at[c], c, 14, mate)]

    def start(copies):
        for copy in copies:
            copy.start()

    def arrived(copies):
        for copy in copies:
            copy.wait_recv()

    load_h.start()

    @pl.loop(0, chunks)
    def _(c):
        for j in range(4):
            load(c, j).start()

    load_h.wait()

    for q in range(NZ):
        hid_t[q] = hid[:, q * block : (q + 1) * block].T

    def stage0(c):
        load(c, 0).wait()

        @pl.loop(0, NZ)
        def _(q):
            term = jnp.dot(hid_t[q], wts[c], preferred_element_type=F32)
            part[c, q] = term.astype(BF16).reshape(NY, rows, width)

        @pl.when(c == 0)
        def _():
            pl.semaphore_wait(barrier, len(peers))

        start(ry_one(c))

    def stage1(c):
        arrived(ry_one(c))
        part[c, lo, yr] = (f32(part[c, lo, yr]) + f32(got1[c, 0])).astype(BF16)
        part[c, hi, yl] = (f32(part[c, hi, yl]) + f32(got1[c, 1])).astype(BF16)
        start(ry_two(c))

    def stage2(c):
        arrived(ry_two(c))
        total = f32(part[c, :, y]) + f32(got2[c, 0]) + f32(got2[c, 1])
        part[c, :, y] = total.astype(BF16)
        start(rz(c))

    def stage3(c):
        load(c, 1).wait()
        arrived(rz(c))
        total = f32(part[c, z, y]) + f32(got3[c, 0])
        total += f32(got3[c, 1]) + f32(got3[c, 2])
        err[c, z, y] = (total - f32(tgt[c])).astype(BF16)
        start(gz(c))

    def stage4(c):
        arrived(gz(c))
        start(gy_one(c))

    def stage5(c):
        arrived(gy_one(c))
        start(gy_two(c))

    def stage6(c):
        arrived(gy_two(c))
        load(c, 2).wait()
        load(c, 3).wait()
        all_err = err[c].reshape(tokens, width)
        grad = jnp.dot(hid[...], all_err, preferred_element_type=F32) * (1.0 / tokens)
        weight = f32(wts[c])
        first = 0.9 * f32(mom[c]) + 0.1 * grad
        second = 0.95 * f32(sec[c]) + 0.05 * grad * grad
        step = (first * (1.0 / corr_first)) / (
            jnp.sqrt(second * (1.0 / corr_second)) + 1e-08
        )
        upd[c] = (weight - 0.02 * (step + 0.1 * weight)).astype(BF16)
        start(swap(c))
        nmo[c] = first.astype(BF16)
        write(c, 0).start()

        @pl.loop(0, NZ)
        def _(q):
            more = lax.dot_general(
                wts[c],
                err[c, q].reshape(block, width),
                (((1,), (1,)), ((), ())),
                preferred_element_type=F32,
            )

            @pl.when(c == 0)
            def _():
                acc[q] = more

            @pl.when(c > 0)
            def _():
                acc[q] += more

        @pl.when(c == last)
        def _():
            for q in range(NZ):
                hgr[:, q * block : (q + 1) * block] = acc[q].astype(BF16)
            write_h.start()

    def stage7(c):
        arrived(swap(c))
        avg[c] = ((f32(upd[c]) + f32(got6[c])) * 0.5).astype(BF16)
        write(c, 1).start()
        for copies in (ry_one, ry_two, rz, gz, gy_one, gy_two, swap):
            for copy in copies(c):
                copy.wait_send()

    stages = [stage0, stage1, stage2, stage3, stage4, stage5, stage6, stage7]

    @pl.loop(0, chunks + len(stages) - 1)
    def _(t):
        for k, stage in enumerate(stages):
            c = t - k

            @pl.when((c >= 0) & (c < chunks))
            def _(c=c, stage=stage):
                stage(c)

    write_h.wait()

    @pl.loop(0, chunks)
    def _(c):
        for j in range(2):
            write(c, j).wait()


def round_at(level, hidden, target, weights, moment, second):
    units, model = weights.shape
    tokens = hidden.shape[1]
    rows = target.shape[0]
    width = min(WIDTH, model)
    chunks = model // width
    block = NY * rows
    whole = jax.ShapeDtypeStruct((units, model), BF16)
    per_chunk = (chunks, units, width)
    return pl.pallas_call(
        functools.partial(kernel, level),
        out_shape=(whole, whole, jax.ShapeDtypeStruct((units, tokens), BF16)),
        in_specs=[pl.BlockSpec(memory_space=pl.ANY)] * 5,
        out_specs=[pl.BlockSpec(memory_space=pl.ANY)] * 3,
        scratch_shapes=[
            pltpu.VMEM((units, tokens), BF16),
            pltpu.VMEM((NZ, block, units), BF16),
            pltpu.VMEM(per_chunk, BF16),
            pltpu.VMEM(per_chunk, BF16),
            pltpu.VMEM(per_chunk, BF16),
            pltpu.VMEM((chunks, rows, width), BF16),
            pltpu.VMEM((chunks, NZ, NY, rows, width), BF16),
            pltpu.VMEM((chunks, 2, NZ // 2, rows, width), BF16),
            pltpu.VMEM((chunks, 2, NZ, rows, width), BF16),
            pltpu.VMEM((chunks, NZ - 1, rows, width), BF16),
            pltpu.VMEM((chunks, NZ, NY, rows, width), BF16),
            pltpu.VMEM((NZ, units, block), F32),
            pltpu.VMEM(per_chunk, BF16),
            pltpu.VMEM(per_chunk, BF16),
            pltpu.VMEM(per_chunk, BF16),
            pltpu.VMEM(per_chunk, BF16),
            pltpu.VMEM((units, tokens), BF16),
            pltpu.SemaphoreType.DMA((chunks, 5)),
            pltpu.SemaphoreType.DMA((chunks, 3)),
            pltpu.SemaphoreType.DMA((chunks, 15)),
            pltpu.SemaphoreType.DMA((chunks, 15)),
        ],
        compiler_params=pltpu.CompilerParams(
            collective_id=level,
            has_side_effects=True,
            vmem_limit_bytes=60 * 1024 * 1024,
        ),
    )(hidden, target, weights, moment, second)


def local(hidden, target, weights, moment, second, round_index):
    levels = 1
    while levels < LEVELS and 2 << levels <= lax.axis_size("rep"):
        levels += 1
    branches = [functools.partial(round_at, level) for level in range(levels)]
    chosen = jnp.remainder(round_index[0], levels)
    averaged, new_moment, hidden_grad = lax.switch(
        chosen, branches, hidden[0], target[0], weights[0], moment[0], second[0]
    )
    return (averaged[None], new_moment[None], hidden_grad[None])


def solution(mesh):
    split = P("rep", "fsdp", None)
    return jax.shard_map(
        local,
        mesh=mesh,
        in_specs=(split,) * 5 + (P(),),
        out_specs=(split,) * 3,
        check_vma=False,
    )
```

time: 305 us -> 166 us (0.54)
  waiting for transfers between devices: 250 us -> 0 us
  Pallas kernels: 0 us -> 159 us
  matrix products: 30.7 us -> 0 us
  between operations: 14.7 us -> 1.31 us
  other arithmetic: 6.13 us -> 0 us
    pallas_call x0 -> x1, Pallas kernels: none -> 159 us  [round_at(): pl.pallas_call(functools.partial(kernel, level), out_shape=(whole, whole,...]
    reduce_scatter x1 -> x0, waiting for transfers between devices: 110 us -> none  [local(): lax.psum_scatter(partial_out.astype(jnp.bfloat16), 'fsdp', scatter_dimens...]
    all_gather x1 -> x0, waiting for transfers between devices: 98.7 us -> none  [local(): all_errors = lax.all_gather(error, 'fsdp', axis=0, tiled=True)]
    ppermute x1 -> x0, waiting for transfers between devices: 40.7 us -> none  [partner(): lax.ppermute(x, axis, [(i, i ^ 1 << bit) for i in range(lax.axis_size(axi...]
    dot_general x3 -> x0, matrix products: 30.7 us -> none  [the longest x1 12.9 us: local(): jnp.dot(hidden_cols, all_errors, preferred_element_type=jnp.float32)]
    broadcast_in_dim x1 -> x0, other arithmetic: 4.17 us -> none  [local(): return (averaged[None], first_new[None], hidden_grad[None])]
  transfers between devices with their start and end apart: 3 -> 0, of which waited for: 3 -> 0; matrix products, arithmetic and copies ran while one was open for 0% -> 0% of each run, Pallas kernels for 0% -> 0%
where the time goes in v1:
time: 166 us
  Pallas kernels  159 us (96%)
  local copies, waits for them, and re-layouts  5.54 us (3%)
    pallas_call x1, Pallas kernels, round_at(): pl.pallas_call(functools.partial(kernel, level), out_shape=(whole, whole,...  159 us
    unnamed x7, local copies, waits for them, and re-layouts  5.54 us

profile of v1, /device:TPU:4, one launch (start us, length us, event | category | flops | bytes accessed | tf_op | source)
XLA Modules:
  0.0 165.5 jit_solution(13147607949623473873)
XLA Ops:
  1.3 158.7 %conditional.1 = ((bf16[448,2048]{1,0:T(8,128)(2,1)S(1)}, bf16[448,2048]{1,0:T(8,128)(2,1)}, bf16[448,2048]{1,0:T(8,128)(2,1)})) conditional(s32[]{:T(128)} %clamp.3, (bf16[448,2048]{1,0:T(8,128)(2,1)}, bf16[128,2048]{1,0:T(8,128)(2,1)}, bf16[448,2048]{1,0:T(8,128)(2,1)}, bf16[448,2048]{1,0:T(8,128)(2,1)}, ...), branch_computations={%region_0.1_spmd, %region_1.2_spmd, %region_2.3_spmd} | conditional | bytes 8 | solution.py:331
  1.3 158.6 %branch_1_fun.1 = (bf16[448,2048]{1,0:T(8,128)(2,1)S(1)}, bf16[448,2048]{1,0:T(8,128)(2,1)}, bf16[448,2048]{1,0:T(8,128)(2,1)}) custom-call(bf16[448,2048]{1,0:T(8,128)(2,1)} %get-tuple-element.50.h_hbm, bf16[128,2048]{1,0:T(8,128)(2,1)} %get-tuple-element.51.t_hbm, bf16[448,2048]{1,0:T(8,128)(2,1)} %get-tuple-element.52.w_hbm, ...), custom_call_target="tpu_custom_call" | custom-call | tf_op jit(solution)/shard_map/cond/branch_1_fun/pallas_call | solution.py:289
  160.0 0.0 copy-start
  160.0 1.2 copy.22
  161.2 0.9 copy-done
  162.1 0.0 copy-start.1
  162.1 1.2 copy.23
  163.4 0.9 copy-done.1
  164.3 1.2 copy.24
Async XLA Ops:
  160.0 2.2 %copy-start = (bf16[448,2048]{1,0:T(8,128)(2,1)S(1)}, bf16[448,2048]{1,0:T(8,128)(2,1)}, u32[]{:S(2)}) copy-start(bf16[448,2048]{1,0:T(8,128)(2,1)} %get-tuple-element.71) | copy-start | bytes 5505028
  162.1 2.2 %copy-start.1 = (bf16[448,2048]{1,0:T(8,128)(2,1)S(1)}, bf16[448,2048]{1,0:T(8,128)(2,1)}, u32[]{:S(2)}) copy-start(bf16[448,2048]{1,0:T(8,128)(2,1)} %get-tuple-element.70) | copy-start | bytes 5505028

commit v2 on v1

--- a/solution.py
+++ b/solution.py
@@ -15,6 +15,7 @@
 NY = 4
 NZ = 4
 WIDTH = 128
+SIDE = 32
 LEVELS = 3
 
 
@@ -41,7 +42,11 @@
     part,
     got1,
     got2,
-    got3,
+    main_got,
+    main_fwd,
+    side_got,
+    side_fwd,
+    got5,
     err,
     acc,
     upd,
@@ -59,6 +64,8 @@
     tokens = NY * NZ * rows
     block = NY * rows
     last = chunks - 1
+    main = pl.ds(0, rows - SIDE)
+    side = pl.ds(rows - SIDE, SIDE)
 
     fs = lax.axis_index("fsdp")
     rep = lax.axis_index("rep")
@@ -71,11 +78,18 @@
     y2 = (y + 2) % NY
     right = {"fsdp": z * NY + yr}
     left = {"fsdp": z * NY + yl}
-    zs = [(z + k) % NZ for k in range(NZ)]
-    zdev = [{"fsdp": zz * NY + y} for zz in zs]
+    end = z % 3 == 0
+    inner = z % 3 > 0
+    near, mid = 1 + z // 3, 2 - z // 3
+    outer, twin, far = 3 * (z - 1), 3 - z, 3 * (2 - z)
+    beyond = pl.ds(2 - 2 * (z // 3), 2)
+    across = pl.ds(4 - 2 * z, 2)
+    ys = [y, yr, y2, yl]
+    ydev = [{"fsdp": z * NY + yy} for yy in ys]
 
     barrier = pltpu.get_barrier_semaphore()
-    peers = [right, left, zdev[1], zdev[2], zdev[3], mate]
+    zpeers = [{"fsdp": (z + k) % NZ * NY + y} for k in range(1, NZ)]
+    peers = [right, left, ydev[2], mate] + zpeers
     for peer in peers:
         pl.semaphore_signal(barrier, inc=1, device_id=peer, device_id_type=MESH)
 
@@ -96,12 +110,12 @@
     load_h = pltpu.make_async_copy(h_hbm, hid, in_sem.at[0, 4])
     write_h = pltpu.make_async_copy(hgr, hg_hbm, out_sem.at[0, 2])
 
-    def remote(src, dst, c, j, dev):
+    def remote(src, dst, c, j, dev, k=None):
         return pltpu.make_async_remote_copy(
             src_ref=src,
             dst_ref=dst,
             send_sem=send_sem.at[c, j],
-            recv_sem=recv_sem.at[c, j],
+            recv_sem=recv_sem.at[c, j if k is None else k],
             device_id=dev,
             device_id_type=MESH,
         )
@@ -111,42 +125,39 @@
 
     def ry_one(c):
         return [
-            remote(part.at[c, lo, y2], got1.at[c, 0], c, 0, right),
-            remote(part.at[c, hi, y2], got1.at[c, 1], c, 1, left),
+            remote(part.at[c, lo, y2, main], got1.at[c, 0], c, 0, right),
+            remote(part.at[c, hi, y2, main], got1.at[c, 1], c, 1, left),
         ]
 
     def ry_two(c):
         return [
-            remote(part.at[c, :, yr], got2.at[c, 0], c, 2, right),
-            remote(part.at[c, :, yl], got2.at[c, 1], c, 3, left),
+            remote(part.at[c, :, yr, main], got2.at[c, 0], c, 2, right),
+            remote(part.at[c, :, yl, main], got2.at[c, 1], c, 3, left),
         ]
 
-    def rz(c):
+    def gy_one(c):
+        own = err.at[c, :, y, main]
+        return [remote(own, own, c, 4, right), remote(own, own, c, 5, left)]
+
+    def gy_two(c):
+        one = err.at[c, lo, yl, main]
+        two = err.at[c, hi, yr, main]
+        return [remote(one, one, c, 6, right), remote(two, two, c, 7, left)]
+
+    def side_ry(c):
         return [
-            remote(part.at[c, zs[k], y], got3.at[c, k - 1], c, 3 + k, zdev[k])
+            remote(part.at[c, z, ys[k], side], got5.at[c, k - 1], c, 8 + k, ydev[k])
             for k in (2, 1, 3)
         ]
 
-    def gz(c):
-        return [
-            remote(err.at[c, z, y], err.at[c, z, y], c, 6 + k, zdev[k])
-            for k in (2, 1, 3)
-        ]
-
-    def gy_one(c):
-        return [
-            remote(err.at[c, :, y], err.at[c, :, y], c, 10, right),
-            remote(err.at[c, :, y], err.at[c, :, y], c, 11, left),
-        ]
-
-    def gy_two(c):
-        return [
-            remote(err.at[c, lo, yl], err.at[c, lo, yl], c, 12, right),
-            remote(err.at[c, hi, yr], err.at[c, hi, yr], c, 13, left),
-        ]
+    def side_gy(c):
+        own = err.at[c, z, y, side]
+        return [remote(own, own, c, 11 + k, ydev[k]) for k in (2, 1, 3)]
 
     def swap(c):
-        return [remote(upd.at[c], got6.at[c], c, 14, mate)]
+        return [remote(upd.at[c], got6.at[c], c, 8, mate)]
+
+    sends = (ry_one, ry_two, gy_one, gy_two, swap, side_ry, side_gy)
 
     def start(copies):
         for copy in copies:
@@ -156,14 +167,134 @@
         for copy in copies:
             copy.wait_recv()
 
+    def zdev(zz):
+        return {"fsdp": zz * NY + y}
+
+    class Line:
+        def __init__(self, view, got, fwd, base):
+            self.view, self.got, self.fwd, self.base = view, got, fwd, base
+
+        def move(self, src, dst, c, j, k, zz):
+            return remote(src, dst, c, self.base + j, zdev(zz), self.base + k)
+
+        def sum_end(self, c):
+            two, one = self.view(part, c, beyond), self.view(part, c, near)
+            return [
+                self.move(two, self.fwd.at[c], c, 0, 0, near),
+                self.move(one, self.got.at[c, 0], c, 1, 1, near),
+            ]
+
+        def sum_inner(self, c):
+            one = self.view(part, c, outer)
+            return [self.move(one, self.got.at[c, 0], c, 1, 1, outer)]
+
+        def sum_on(self, c):
+            one, two = self.view(part, c, far), self.view(part, c, twin)
+            return [
+                self.move(one, self.got.at[c, 1], c, 3, 2, far),
+                self.move(two, self.got.at[c, 1], c, 2, 2, twin),
+            ]
+
+        def sum_start(self, c):
+            @pl.when(end)
+            def _():
+                start(self.sum_end(c))
+
+            @pl.when(inner)
+            def _():
+                start(self.sum_inner(c))
+
+        def sum_forward(self, c):
+            @pl.when(inner)
+            def _():
+                two = self.view(part, c, across)
+                self.move(two, self.fwd.at[c], c, 0, 0, outer).wait_recv()
+                two[...] = (f32(two[...]) + f32(self.fwd[c])).astype(BF16)
+                start(self.sum_on(c))
+
+        def sum_finish(self, c):
+            own = self.view(part, c, z)
+            for k in range(2):
+                got = self.got.at[c, k]
+                self.move(got, got, c, 1 + k, 1 + k, twin).wait_recv()
+            return f32(own[...]) + f32(self.got[c, 0]) + f32(self.got[c, 1])
+
+        def share_end(self, c):
+            own = self.view(err, c, z)
+            return [
+                self.move(own, own, c, 4, 6, mid),
+                self.move(own, own, c, 5, 4, near),
+            ]
+
+        def share_inner(self, c):
+            own = self.view(err, c, z)
+            return [
+                self.move(own, own, c, 4, 5, twin),
+                self.move(own, own, c, 5, 4, outer),
+            ]
+
+        def share_on(self, c):
+            two = self.view(err, c, across)
+            return [self.move(two, two, c, 6, 7, outer)]
+
+        def share_start(self, c):
+            @pl.when(end)
+            def _():
+                start(self.share_end(c))
+
+            @pl.when(inner)
+            def _():
+                start(self.share_inner(c))
+
+        def share_forward(self, c):
+            own = self.view(err, c, z)
+            self.move(own, own, c, 4, 4, twin).wait_recv()
+
+            @pl.when(inner)
+            def _():
+                for k in (5, 6):
+                    self.move(own, own, c, 4, k, twin).wait_recv()
+                start(self.share_on(c))
+
+        def share_finish(self, c):
+            @pl.when(end)
+            def _():
+                two = self.view(err, c, beyond)
+                self.move(two, two, c, 6, 7, twin).wait_recv()
+
+        def sent(self, c):
+            @pl.when(end)
+            def _():
+                for copy in self.sum_end(c) + self.share_end(c):
+                    copy.wait_send()
+
+            @pl.when(inner)
+            def _():
+                copies = self.sum_inner(c) + self.sum_on(c)
+                for copy in copies + self.share_inner(c) + self.share_on(c):
+                    copy.wait_send()
+
+    def main_view(ref, c, zz):
+        return ref.at[c, zz, y, main]
+
+    def side_view(ref, c, zz):
+        return ref.at[c, zz, :, side]
+
+    main_line = Line(main_view, main_got, main_fwd, 15)
+    side_line = Line(side_view, side_got, side_fwd, 23)
+
     load_h.start()
+    load(0, 0).start()
+    load_h.wait()
+
+    @pl.loop(1, chunks)
+    def _(c):
+        load(c, 0).start()
 
     @pl.loop(0, chunks)
     def _(c):
-        for j in range(4):
+        for j in range(1, 4):
             load(c, j).start()
-
-    load_h.wait()
 
     for q in range(NZ):
         hid_t[q] = hid[:, q * block : (q + 1) * block].T
@@ -181,36 +312,54 @@
             pl.semaphore_wait(barrier, len(peers))
 
         start(ry_one(c))
+        side_line.sum_start(c)
 
     def stage1(c):
         arrived(ry_one(c))
-        part[c, lo, yr] = (f32(part[c, lo, yr]) + f32(got1[c, 0])).astype(BF16)
-        part[c, hi, yl] = (f32(part[c, hi, yl]) + f32(got1[c, 1])).astype(BF16)
+        part[c, lo, yr, main] = (f32(part[c, lo, yr, main]) + f32(got1[c, 0])).astype(BF16)
+        part[c, hi, yl, main] = (f32(part[c, hi, yl, main]) + f32(got1[c, 1])).astype(BF16)
         start(ry_two(c))
+        side_line.sum_forward(c)
 
     def stage2(c):
+        total = side_line.sum_finish(c)
+        part[c, z, :, side] = total.astype(BF16)
+        start(side_ry(c))
         arrived(ry_two(c))
-        total = f32(part[c, :, y]) + f32(got2[c, 0]) + f32(got2[c, 1])
-        part[c, :, y] = total.astype(BF16)
-        start(rz(c))
+        total = f32(part[c, :, y, main]) + f32(got2[c, 0]) + f32(got2[c, 1])
+        part[c, :, y, main] = total.astype(BF16)
+        main_line.sum_start(c)
 
     def stage3(c):
         load(c, 1).wait()
-        arrived(rz(c))
-        total = f32(part[c, z, y]) + f32(got3[c, 0])
-        total += f32(got3[c, 1]) + f32(got3[c, 2])
-        err[c, z, y] = (total - f32(tgt[c])).astype(BF16)
-        start(gz(c))
+        arrived(side_ry(c))
+        total = f32(part[c, z, y, side]) + f32(got5[c, 0])
+        total += f32(got5[c, 1]) + f32(got5[c, 2])
+        err[c, z, y, side] = (total - f32(tgt[c, side])).astype(BF16)
+        start(side_gy(c))
+        main_line.sum_forward(c)
 
     def stage4(c):
-        arrived(gz(c))
+        arrived(side_gy(c))
+        side_line.share_start(c)
+        total = main_line.sum_finish(c)
+        err[c, z, y, main] = (total - f32(tgt[c, main])).astype(BF16)
+        main_line.share_start(c)
+
+    def stage5(c):
+        side_line.share_forward(c)
+        main_line.share_forward(c)
+
+    def stage6(c):
+        main_line.share_finish(c)
         start(gy_one(c))
 
-    def stage5(c):
+    def stage7(c):
         arrived(gy_one(c))
         start(gy_two(c))
 
-    def stage6(c):
+    def stage8(c):
+        side_line.share_finish(c)
         arrived(gy_two(c))
         load(c, 2).wait()
         load(c, 3).wait()
@@ -250,20 +399,33 @@
                 hgr[:, q * block : (q + 1) * block] = acc[q].astype(BF16)
             write_h.start()
 
-    def stage7(c):
+    def stage9(c):
         arrived(swap(c))
         avg[c] = ((f32(upd[c]) + f32(got6[c])) * 0.5).astype(BF16)
         write(c, 1).start()
-        for copies in (ry_one, ry_two, rz, gz, gy_one, gy_two, swap):
+        main_line.sent(c)
+        side_line.sent(c)
+        for copies in sends:
             for copy in copies(c):
                 copy.wait_send()
 
-    stages = [stage0, stage1, stage2, stage3, stage4, stage5, stage6, stage7]
-
-    @pl.loop(0, chunks + len(stages) - 1)
+    stages = (
+        (0, stage0),
+        (2, stage1),
+        (4, stage2),
+        (6, stage3),
+        (8, stage4),
+        (10, stage5),
+        (12, stage6),
+        (14, stage7),
+        (16, stage8),
+        (18, stage9),
+    )
+
+    @pl.loop(0, chunks + stages[-1][0])
     def _(t):
-        for k, stage in enumerate(stages):
-            c = t - k
+        for lag, stage in stages:
+            c = t - lag
 
             @pl.when((c >= 0) & (c < chunks))
             def _(c=c, stage=stage):
@@ -299,9 +461,13 @@
             pltpu.VMEM(per_chunk, BF16),
             pltpu.VMEM((chunks, rows, width), BF16),
             pltpu.VMEM((chunks, NZ, NY, rows, width), BF16),
-            pltpu.VMEM((chunks, 2, NZ // 2, rows, width), BF16),
-            pltpu.VMEM((chunks, 2, NZ, rows, width), BF16),
-            pltpu.VMEM((chunks, NZ - 1, rows, width), BF16),
+            pltpu.VMEM((chunks, 2, NZ // 2, rows - SIDE, width), BF16),
+            pltpu.VMEM((chunks, 2, NZ, rows - SIDE, width), BF16),
+            pltpu.VMEM((chunks, 2, rows - SIDE, width), BF16),
+            pltpu.VMEM((chunks, 2, rows - SIDE, width), BF16),
+            pltpu.VMEM((chunks, 2, NY, SIDE, width), BF16),
+            pltpu.VMEM((chunks, 2, NY, SIDE, width), BF16),
+            pltpu.VMEM((chunks, NY - 1, SIDE, width), BF16),
             pltpu.VMEM((chunks, NZ, NY, rows, width), BF16),
             pltpu.VMEM((NZ, units, block), F32),
             pltpu.VMEM(per_chunk, BF16),
@@ -311,13 +477,13 @@
             pltpu.VMEM((units, tokens), BF16),
             pltpu.SemaphoreType.DMA((chunks, 5)),
             pltpu.SemaphoreType.DMA((chunks, 3)),
-            pltpu.SemaphoreType.DMA((chunks, 15)),
-            pltpu.SemaphoreType.DMA((chunks, 15)),
+            pltpu.SemaphoreType.DMA((chunks, 31)),
+            pltpu.SemaphoreType.DMA((chunks, 31)),
         ],
         compiler_params=pltpu.CompilerParams(
             collective_id=level,
             has_side_effects=True,
-            vmem_limit_bytes=60 * 1024 * 1024,
+            vmem_limit_bytes=50 * 1024 * 1024,
         ),
     )(hidden, target, weights, moment, second)
 

time: 166 us -> 148 us (0.89)
  Pallas kernels: 159 us -> 142 us
  local copies, waits for them, and re-layouts: 5.54 us -> 3.69 us
    pallas_call x1, Pallas kernels: 159 us -> 142 us  [round_at(): pl.pallas_call(functools.partial(kernel, level), out_shape=(whole, whole,...]
    unnamed x7 -> x3, local copies, waits for them, and re-layouts: 5.54 us -> 3.69 us
where the time goes in v2:
time: 148 us
  Pallas kernels  142 us (96%)
  local copies, waits for them, and re-layouts  3.69 us (2%)
    pallas_call x1, Pallas kernels, round_at(): pl.pallas_call(functools.partial(kernel, level), out_shape=(whole, whole,...  142 us
    unnamed x3, local copies, waits for them, and re-layouts  3.69 us

profile of v2, /device:TPU:4, one launch (start us, length us, event | category | flops | bytes accessed | tf_op | source)
XLA Modules:
  0.0 147.6 jit_solution(9047372117434213274)
XLA Ops:
  1.3 142.6 %conditional.1 = ((bf16[448,2048]{1,0:T(8,128)(2,1)S(1)}, bf16[448,2048]{1,0:T(8,128)(2,1)S(1)}, bf16[448,2048]{1,0:T(8,128)(2,1)S(1)})) conditional(s32[]{:T(128)} %clamp.3, (bf16[448,2048]{1,0:T(8,128)(2,1)}, bf16[128,2048]{1,0:T(8,128)(2,1)}, bf16[448,2048]{1,0:T(8,128)(2,1)}, bf16[448,2048]{1,0:T(8,128)(2,1)}, ...), branch_computations={%region_0.1_spmd, %region_1.2_spmd, %region_2.3_spmd} | conditional | bytes 8 | solution.py:497
  1.3 142.3 %branch_0_fun.1 = (bf16[448,2048]{1,0:T(8,128)(2,1)S(1)}, bf16[448,2048]{1,0:T(8,128)(2,1)S(1)}, bf16[448,2048]{1,0:T(8,128)(2,1)S(1)}) custom-call(bf16[448,2048]{1,0:T(8,128)(2,1)} %get-tuple-element.42.h_hbm, bf16[128,2048]{1,0:T(8,128)(2,1)} %get-tuple-element.43.t_hbm, bf16[448,2048]{1,0:T(8,128)(2,1)} %get-tuple-element.44.w_hbm, ...), custom_call_target="tpu_custom_call" | custom-call | tf_op jit(solution)/shard_map/cond/branch_0_fun/pallas_call | solution.py:451
  143.9 1.2 copy.22
  145.1 1.2 copy.23
  146.4 1.2 copy.24

commit v3 on v2

--- a/solution.py
+++ b/solution.py
@@ -14,7 +14,7 @@
 corr_second = 0.994079470779666
 NY = 4
 NZ = 4
-WIDTH = 128
+WIDTH = 256
 SIDE = 32
 LEVELS = 3
 
@@ -49,6 +49,7 @@
     got5,
     err,
     acc,
+    gsum,
     upd,
     got6,
     avg,
@@ -107,7 +108,10 @@
         src, dst = sinks[j]
         return pltpu.make_async_copy(src.at[c], dst.at[:, cols(c)], out_sem.at[c, j])
 
-    load_h = pltpu.make_async_copy(h_hbm, hid, in_sem.at[0, 4])
+    def load_h(q):
+        some = pl.ds(q * block, block)
+        return pltpu.make_async_copy(h_hbm.at[:, some], hid.at[:, some], in_sem.at[q, 4])
+
     write_h = pltpu.make_async_copy(hgr, hg_hbm, out_sem.at[0, 2])
 
     def remote(src, dst, c, j, dev, k=None):
@@ -154,8 +158,14 @@
         own = err.at[c, z, y, side]
         return [remote(own, own, c, 11 + k, ydev[k]) for k in (2, 1, 3)]
 
+    half = units // 2
+    halves = [pl.ds(0, half), pl.ds(half, half)]
+
     def swap(c):
-        return [remote(upd.at[c], got6.at[c], c, 8, mate)]
+        return [
+            remote(upd.at[c, part_rows], got6.at[c, part_rows], c, j, mate)
+            for part_rows, j in zip(halves, (8, 31))
+        ]
 
     sends = (ry_one, ry_two, gy_one, gy_two, swap, side_ry, side_gy)
 
@@ -283,9 +293,9 @@
     main_line = Line(main_view, main_got, main_fwd, 15)
     side_line = Line(side_view, side_got, side_fwd, 23)
 
-    load_h.start()
     load(0, 0).start()
-    load_h.wait()
+    for q in range(NZ):
+        load_h(q).start()
 
     @pl.loop(1, chunks)
     def _(c):
@@ -296,11 +306,14 @@
         for j in range(1, 4):
             load(c, j).start()
 
-    for q in range(NZ):
-        hid_t[q] = hid[:, q * block : (q + 1) * block].T
-
     def stage0(c):
         load(c, 0).wait()
+
+        @pl.when(c == 0)
+        def _():
+            for q in range(NZ):
+                load_h(q).wait()
+                hid_t[q] = hid[:, q * block : (q + 1) * block].T
 
         @pl.loop(0, NZ)
         def _(q):
@@ -364,35 +377,33 @@
         load(c, 2).wait()
         load(c, 3).wait()
         all_err = err[c].reshape(tokens, width)
-        grad = jnp.dot(hid[...], all_err, preferred_element_type=F32) * (1.0 / tokens)
-        weight = f32(wts[c])
-        first = 0.9 * f32(mom[c]) + 0.1 * grad
-        second = 0.95 * f32(sec[c]) + 0.05 * grad * grad
-        step = (first * (1.0 / corr_first)) / (
-            jnp.sqrt(second * (1.0 / corr_second)) + 1e-08
-        )
-        upd[c] = (weight - 0.02 * (step + 0.1 * weight)).astype(BF16)
-        start(swap(c))
-        nmo[c] = first.astype(BF16)
+        for move, some in zip(swap(c), halves):
+            grad = jnp.dot(hid[some], all_err, preferred_element_type=F32)
+            grad = grad * (1.0 / tokens)
+            weight = f32(wts[c, some])
+            first = 0.9 * f32(mom[c, some]) + 0.1 * grad
+            second = 0.95 * f32(sec[c, some]) + 0.05 * grad * grad
+            step = (first * (1.0 / corr_first)) / (
+                jnp.sqrt(second * (1.0 / corr_second)) + 1e-08
+            )
+            upd[c, some] = (weight - 0.02 * (step + 0.1 * weight)).astype(BF16)
+            move.start()
+            nmo[c, some] = first.astype(BF16)
         write(c, 0).start()
+
+        @pl.when(c == 0)
+        def _():
+            acc[...] = jnp.zeros_like(acc)
 
         @pl.loop(0, NZ)
         def _(q):
-            more = lax.dot_general(
+            acc[q] += lax.dot_general(
                 wts[c],
                 err[c, q].reshape(block, width),
                 (((1,), (1,)), ((), ())),
                 preferred_element_type=F32,
             )
 
-            @pl.when(c == 0)
-            def _():
-                acc[q] = more
-
-            @pl.when(c > 0)
-            def _():
-                acc[q] += more
-
         @pl.when(c == last)
         def _():
             for q in range(NZ):
@@ -400,8 +411,10 @@
             write_h.start()
 
     def stage9(c):
-        arrived(swap(c))
-        avg[c] = ((f32(upd[c]) + f32(got6[c])) * 0.5).astype(BF16)
+        for move, some in zip(swap(c), halves):
+            move.wait_recv()
+            both = f32(upd[c, some]) + f32(got6[c, some])
+            avg[c, some] = (both * 0.5).astype(BF16)
         write(c, 1).start()
         main_line.sent(c)
         side_line.sent(c)
@@ -411,18 +424,18 @@
 
     stages = (
         (0, stage0),
-        (2, stage1),
-        (4, stage2),
-        (6, stage3),
-        (8, stage4),
-        (10, stage5),
-        (12, stage6),
-        (14, stage7),
-        (16, stage8),
-        (18, stage9),
+        (1, stage1),
+        (2, stage2),
+        (3, stage3),
+        (4, stage4),
+        (5, stage5),
+        (6, stage6),
+        (7, stage7),
+        (8, stage8),
+        (9, stage9),
     )
 
-    @pl.loop(0, chunks + stages[-1][0])
+    @pl.loop(0, chunks + 9)
     def _(t):
         for lag, stage in stages:
             c = t - lag
@@ -470,15 +483,16 @@
             pltpu.VMEM((chunks, NY - 1, SIDE, width), BF16),
             pltpu.VMEM((chunks, NZ, NY, rows, width), BF16),
             pltpu.VMEM((NZ, units, block), F32),
+            pltpu.VMEM((units, width), F32),
             pltpu.VMEM(per_chunk, BF16),
             pltpu.VMEM(per_chunk, BF16),
             pltpu.VMEM(per_chunk, BF16),
             pltpu.VMEM(per_chunk, BF16),
             pltpu.VMEM((units, tokens), BF16),
-            pltpu.SemaphoreType.DMA((chunks, 5)),
+            pltpu.SemaphoreType.DMA((max(chunks, NZ), 5)),
             pltpu.SemaphoreType.DMA((chunks, 3)),
-            pltpu.SemaphoreType.DMA((chunks, 31)),
-            pltpu.SemaphoreType.DMA((chunks, 31)),
+            pltpu.SemaphoreType.DMA((chunks, 32)),
+            pltpu.SemaphoreType.DMA((chunks, 32)),
         ],
         compiler_params=pltpu.CompilerParams(
             collective_id=level,

time: 148 us -> 148 us (level)
  no operation moved by 1% of the time
where the time goes in v3:
time: 148 us; the launch traced here: 147 us
  Pallas kernels  142 us (96%)
  local copies, waits for them, and re-layouts  3.69 us (2%)
    pallas_call x1, Pallas kernels, round_at(): pl.pallas_call(functools.partial(kernel, level), out_shape=(whole, whole,...  142 us
    unnamed x3, local copies, waits for them, and re-layouts  3.69 us

profile of v3, /device:TPU:4, one launch (start us, length us, event | category | flops | bytes accessed | tf_op | source)
XLA Modules:
  0.0 147.5 jit_solution(13912257438763460290)
XLA Ops:
  1.3 142.5 %conditional.1 = ((bf16[448,2048]{1,0:T(8,128)(2,1)S(1)}, bf16[448,2048]{1,0:T(8,128)(2,1)S(1)}, bf16[448,2048]{1,0:T(8,128)(2,1)S(1)})) conditional(s32[]{:T(128)} %clamp.3, (bf16[448,2048]{1,0:T(8,128)(2,1)}, bf16[128,2048]{1,0:T(8,128)(2,1)}, bf16[448,2048]{1,0:T(8,128)(2,1)}, bf16[448,2048]{1,0:T(8,128)(2,1)}, ...), branch_computations={%region_0.1_spmd, %region_1.2_spmd, %region_2.3_spmd} | conditional | bytes 8 | solution.py:511
  1.3 142.0 %branch_1_fun.1 = (bf16[448,2048]{1,0:T(8,128)(2,1)S(1)}, bf16[448,2048]{1,0:T(8,128)(2,1)S(1)}, bf16[448,2048]{1,0:T(8,128)(2,1)S(1)}) custom-call(bf16[448,2048]{1,0:T(8,128)(2,1)} %get-tuple-element.50.h_hbm, bf16[128,2048]{1,0:T(8,128)(2,1)} %get-tuple-element.51.t_hbm, bf16[448,2048]{1,0:T(8,128)(2,1)} %get-tuple-element.52.w_hbm, ...), custom_call_target="tpu_custom_call" | custom-call | tf_op jit(solution)/shard_map/cond/branch_1_fun/pallas_call | solution.py:464
  143.8 1.2 copy.22
  145.0 1.2 copy.23
  146.2 1.2 copy.24

commit v4 on v3

--- a/solution.py
+++ b/solution.py
@@ -315,16 +315,20 @@
                 load_h(q).wait()
                 hid_t[q] = hid[:, q * block : (q + 1) * block].T
 
-        @pl.loop(0, NZ)
-        def _(q):
+        def terms(q):
             term = jnp.dot(hid_t[q], wts[c], preferred_element_type=F32)
             part[c, q] = term.astype(BF16).reshape(NY, rows, width)
+
+        one, two = ry_one(c)
+        pl.loop(0, NZ // 2)(terms)
 
         @pl.when(c == 0)
         def _():
             pl.semaphore_wait(barrier, len(peers))
 
-        start(ry_one(c))
+        one.start()
+        pl.loop(NZ // 2, NZ)(terms)
+        two.start()
         side_line.sum_start(c)
 
     def stage1(c):
@@ -376,10 +380,11 @@
         arrived(gy_two(c))
         load(c, 2).wait()
         load(c, 3).wait()
-        all_err = err[c].reshape(tokens, width)
+        gsum[...] = jnp.dot(
+            hid[...], err[c].reshape(tokens, width), preferred_element_type=F32
+        )
         for move, some in zip(swap(c), halves):
-            grad = jnp.dot(hid[some], all_err, preferred_element_type=F32)
-            grad = grad * (1.0 / tokens)
+            grad = gsum[some] * (1.0 / tokens)
             weight = f32(wts[c, some])
             first = 0.9 * f32(mom[c, some]) + 0.1 * grad
             second = 0.95 * f32(sec[c, some]) + 0.05 * grad * grad

time: 148 us -> 148 us (level)
  no operation moved by 1% of the time
where the time goes in v4:
time: 148 us; the launch traced here: 146 us
  Pallas kernels  141 us (95%)
  local copies, waits for them, and re-layouts  3.69 us (2%)
    pallas_call x1, Pallas kernels, round_at(): pl.pallas_call(functools.partial(kernel, level), out_shape=(whole, whole,...  141 us
    unnamed x3, local copies, waits for them, and re-layouts  3.69 us

profile of v4, /device:TPU:4, one launch (start us, length us, event | category | flops | bytes accessed | tf_op | source)
XLA Modules:
  0.0 146.4 jit_solution(17191896163591271947)
XLA Ops:
  1.3 141.4 %conditional.1 = ((bf16[448,2048]{1,0:T(8,128)(2,1)S(1)}, bf16[448,2048]{1,0:T(8,128)(2,1)S(1)}, bf16[448,2048]{1,0:T(8,128)(2,1)S(1)})) conditional(s32[]{:T(128)} %clamp.3, (bf16[448,2048]{1,0:T(8,128)(2,1)}, bf16[128,2048]{1,0:T(8,128)(2,1)}, bf16[448,2048]{1,0:T(8,128)(2,1)}, bf16[448,2048]{1,0:T(8,128)(2,1)}, ...), branch_computations={%region_0.1_spmd, %region_1.2_spmd, %region_2.3_spmd} | conditional | bytes 8 | solution.py:516
  1.5 141.0 %branch_2_fun.1 = (bf16[448,2048]{1,0:T(8,128)(2,1)S(1)}, bf16[448,2048]{1,0:T(8,128)(2,1)S(1)}, bf16[448,2048]{1,0:T(8,128)(2,1)S(1)}) custom-call(bf16[448,2048]{1,0:T(8,128)(2,1)} %get-tuple-element.58.h_hbm, bf16[128,2048]{1,0:T(8,128)(2,1)} %get-tuple-element.59.t_hbm, bf16[448,2048]{1,0:T(8,128)(2,1)} %get-tuple-element.60.w_hbm, ...), custom_call_target="tpu_custom_call" | custom-call | tf_op jit(solution)/shard_map/cond/branch_2_fun/pallas_call | solution.py:469
  142.7 1.2 copy.22
  144.0 1.2 copy.23
  145.2 1.2 copy.24
